TPU v7x, 32 devices: a whole 2x2x4 slice. The times are simulated.
32 devices in a mesh: lat: 8 (over y, x, core), lon: 4 (over z).
Axes of the slice: x: 2, y: 2, z: 4, core: 2. Of those that a mesh axis runs over, the one named last changes fastest.
Arguments:
- gaussian_thermal_state: float32 [16, 1280, 2560], P(None, 'lat', 'lon'), may hold values from -6 to 6
- radiation_holder_device: int32 [32, 25600, 1], P(('lat', 'lon')), may hold values from 0 to 31; in each aligned block of 25600 rows (0 to 25599, 25600 to 51199, ..., all dimensions but the last counted through in order) at most 1280 rows name the same one
- layer_opacity_depths: bfloat16 [32, 16, 16, 40960], P(('lat', 'lon')), may hold values from 0.049804688 to 3
- wavenumber_duos_placed: int32 [640], replicated, may hold values from 0 to 639, each once
- reduced_grid_sites: int32 [1280], P('lat'), may hold values from 640 to 2560
- weighted_polynomial_basis: bfloat16 [640, 1280, 1344], P(('lat', 'lon')), may hold values from -0.15625 to 0.15625
Outputs:
- new_temperature: float32 [16, 1280, 2560], P(None, 'lat', 'lon')
Inputs may be any that keep to these rules, and one draw needn't show every extreme that they name: `radiation_holder_device`: in each block d no owner is named by more than 1280 of the block's 25600 columns; some owner is named by exactly 1280 in some blocks. `wavenumber_duos_placed`: each pair number appears in exactly one slot.
All inputs are finite; a program needn't handle non-finite values.
Results may differ from a plain program's by a relative error of at most 0.0072.
Values may be sent and summed in bfloat16 or wider, within the bound.
A program may use at most 448 MiB of HBM per device.

v0:
```python
import math

import jax
import jax.numpy as jnp
from jax import lax
from jax.sharding import PartitionSpec as P

DIFFUSION = 4.0


def wave_numbers(pairs, nwave):
    repeated = jnp.repeat(pairs, 4)
    which = jnp.tile(jnp.array([0, 0, 1, 1], dtype=jnp.int32), pairs.shape[0])
    return jnp.where(which == 0, repeated, nwave - 1 - repeated)


def dft_table(waves, nlon):
    places = jnp.arange(nlon, dtype=jnp.int32)
    phase = places[:, None] * waves[None, :] % nlon
    angle = phase.astype(jnp.float32) * (2.0 * math.pi / nlon)
    parity = jnp.arange(waves.shape[0], dtype=jnp.int32) % 2
    values = jnp.where(parity[None, :] == 0, jnp.cos(angle), jnp.sin(angle))
    return (values * (1.0 / math.sqrt(nlon))).astype(jnp.bfloat16)


def owner_ranks(owner, devices_all):
    matches = (owner[:, None] == jnp.arange(devices_all, dtype=jnp.int32)[None, :]).astype(
        jnp.int32
    )
    counts = jnp.sum(matches, axis=0)
    starts = jnp.cumsum(counts) - counts
    start_each = jnp.sum(matches * starts[None, :], axis=1)
    order = jnp.argsort(owner, stable=True)
    position = jnp.zeros_like(owner).at[order].set(jnp.arange(owner.shape[0], dtype=jnp.int32))
    return position - start_each


def flux_step(flux, inputs):
    passing, planck = inputs
    fresh = passing * flux + (1.0 - passing) * planck
    return (fresh, fresh)


def radiate(column_temp, depth):
    bands = depth.shape[1]
    source = jnp.exp(0.5 * column_temp.astype(jnp.float32))
    weights = (jnp.arange(bands, dtype=jnp.float32) + 1.0) * (2.0 / (bands * (bands + 1)))
    passing = jnp.exp(-depth.astype(jnp.float32))
    planck = weights[None, :, None] * source[:, None, :]
    _, below = lax.scan(flux_step, jnp.zeros_like(planck[0]), (passing, planck))
    above = jnp.concatenate([jnp.zeros_like(planck[:1]), below[:-1]], axis=0)
    _, upper = lax.scan(flux_step, planck[-1], (passing, planck), reverse=True)
    under = jnp.concatenate([upper[1:], planck[-1:]], axis=0)
    return jnp.sum(above - below + under - upper, axis=1)


def per_device(
    gaussian_thermal_state,
    radiation_holder_device,
    layer_opacity_depths,
    wavenumber_duos_placed,
    reduced_grid_sites,
    weighted_polynomial_basis,
):
    vertical_layer_pile, parallel_circle_lines, meridian_entries = gaussian_thermal_state.shape
    group = weighted_polynomial_basis.shape[0]
    nlat_all = weighted_polynomial_basis.shape[1]
    ndeg = weighted_polynomial_basis.shape[2]
    nwave = wavenumber_duos_placed.shape[0] * 2
    nlon = nwave * 2
    lat_size = lax.axis_size("lat")
    lon_size = lax.axis_size("lon")
    devices_all = lat_size * lon_size
    capacity = layer_opacity_depths.shape[3] // devices_all
    level_group = vertical_layer_pile // lon_size
    reduced_resolution_grid = (
        gaussian_thermal_state[:, 0::2, 0::2]
        + gaussian_thermal_state[:, 1::2, 0::2]
        + (gaussian_thermal_state[:, 0::2, 1::2] + gaussian_thermal_state[:, 1::2, 1::2])
    ) * 0.25
    coarse_rows, coarse_cols = (reduced_resolution_grid.shape[1], reduced_resolution_grid.shape[2])
    column_temp = reduced_resolution_grid.astype(jnp.bfloat16).reshape(
        vertical_layer_pile, coarse_rows * coarse_cols
    )
    owner = radiation_holder_device[0, :, 0]
    slots = owner * capacity + owner_ranks(owner, devices_all)
    outgoing = (
        jnp.zeros((vertical_layer_pile, devices_all * capacity), jnp.bfloat16)
        .at[:, slots]
        .set(column_temp)
    )
    arrived = lax.all_to_all(
        outgoing.reshape(vertical_layer_pile, devices_all, capacity),
        ("lat", "lon"),
        split_axis=1,
        concat_axis=1,
        tiled=True,
    )
    heating = radiate(
        arrived.reshape(vertical_layer_pile, devices_all * capacity), layer_opacity_depths[0]
    ).astype(jnp.bfloat16)
    returned = lax.all_to_all(
        heating.reshape(vertical_layer_pile, devices_all, capacity),
        ("lat", "lon"),
        split_axis=1,
        concat_axis=1,
        tiled=True,
    )
    column_heat = returned.reshape(vertical_layer_pile, devices_all * capacity)[:, slots].reshape(
        vertical_layer_pile, coarse_rows, coarse_cols
    )
    full_resolution_warming = jnp.repeat(jnp.repeat(column_heat, 2, axis=1), 2, axis=2)
    radiatively_driven_thermal = (
        gaussian_thermal_state + full_resolution_warming.astype(jnp.float32)
    ).astype(jnp.bfloat16)
    all_waves = wave_numbers(wavenumber_duos_placed, nwave)
    full_table = dft_table(all_waves, nlon)
    piece = lax.all_to_all(
        radiatively_driven_thermal, "lon", split_axis=0, concat_axis=2, tiled=True
    )
    product = jnp.dot(piece.reshape(-1, nlon), full_table, preferred_element_type=jnp.float32)
    row_spectra = product.reshape(piece.shape[0], piece.shape[1], full_table.shape[1])
    keep_all = 2 * all_waves[None, :] < reduced_grid_sites[:, None]
    row_fourier = jnp.where(keep_all[None], row_spectra, 0.0).astype(jnp.bfloat16)
    sending = row_fourier.reshape(
        level_group, parallel_circle_lines, lat_size, lon_size, 4 * group
    ).transpose(2, 3, 0, 1, 4)
    flat_send = sending.reshape(devices_all, level_group, parallel_circle_lines, 4 * group)
    gathered = lax.all_to_all(
        flat_send, ("lat", "lon"), split_axis=0, concat_axis=0, tiled=True
    ).reshape(lat_size, lon_size, level_group, parallel_circle_lines, 4 * group)
    fourier = gathered.transpose(1, 2, 0, 3, 4).reshape(vertical_layer_pile, nlat_all, group, 2, 2)
    device_index = lax.axis_index("lat") * lon_size + lax.axis_index("lon")
    my_pairs = lax.dynamic_slice_in_dim(wavenumber_duos_placed, device_index * group, group)
    full = jnp.einsum(
        "syc,lyswp->cswlp", weighted_polynomial_basis, fourier, preferred_element_type=jnp.float32
    )
    coeff = jnp.arange(ndeg, dtype=jnp.int32)
    first = coeff[:, None] < (nwave - my_pairs)[None, :]
    chosen = jnp.where(first[:, :, None, None], full[:, :, 0], full[:, :, 1])
    degree = jnp.where(first, my_pairs[None, :] + coeff[:, None], coeff[:, None] - 1).astype(
        jnp.float32
    )
    factor = jnp.where(
        coeff[:, None] <= nwave,
        1.0 / (1.0 + DIFFUSION * degree * (degree + 1.0) / (nwave * nwave)),
        0.0,
    )
    damped = (chosen * factor[:, :, None, None]).astype(jnp.bfloat16)
    blank = jnp.zeros_like(damped)
    first_mask = first[:, :, None, None]
    split = jnp.stack(
        [jnp.where(first_mask, damped, blank), jnp.where(first_mask, blank, damped)], axis=2
    )
    synth = jnp.einsum(
        "syc,cswlp->lyswp", weighted_polynomial_basis, split, preferred_element_type=jnp.float32
    )
    synth = synth.astype(jnp.bfloat16)
    back_rows = synth.reshape(
        lon_size, level_group, lat_size, parallel_circle_lines, 4 * group
    ).transpose(2, 0, 1, 3, 4)
    came_back = lax.all_to_all(
        back_rows.reshape(devices_all, level_group, parallel_circle_lines, 4 * group),
        ("lat", "lon"),
        split_axis=0,
        concat_axis=0,
        tiled=True,
    )
    row_synth = came_back.transpose(1, 2, 0, 3).reshape(
        level_group * parallel_circle_lines, devices_all * 4 * group
    )
    lat_grid = lax.dot_general(
        row_synth, full_table, (((1,), (1,)), ((), ())), preferred_element_type=jnp.float32
    )
    lat_grid = lat_grid.reshape(level_group, parallel_circle_lines, nlon)
    return lax.all_to_all(lat_grid, "lon", split_axis=2, concat_axis=0, tiled=True)


def solution(mesh):
    in_specs = (
        P(None, "lat", "lon"),
        P(("lat", "lon"), None, None),
        P(("lat", "lon"), None, None, None),
        P(),
        P("lat"),
        P(("lat", "lon"), None, None),
    )
    out_specs = P(None, "lat", "lon")
    return jax.shard_map(
        per_device, mesh=mesh, in_specs=in_specs, out_specs=out_specs, check_vma=False
    )
```

profile of v0, /device:TPU:0, one launch (start us, length us, event | category | flops | bytes accessed | tf_op | source)
XLA Modules:
  0.0 1915.3 jit_solution(16173581751223085848)
XLA Ops:
  0.0 56.1 %slice.28 = f32[16,80,320]{2,1,0:T(8,128)S(1)} slice(f32[16,160,640]{2,1,0:T(8,128)} %param.11), slice={[0:16:1], [0:160:2], [0:640:2]} | slice | bytes 3276800 | tf_op jit(solution)/shard_map/slice | solution.py:77
  56.1 56.5 %slice.29 = f32[16,80,320]{2,1,0:T(8,128)} slice(f32[16,160,640]{2,1,0:T(8,128)} %param.11), slice={[0:16:1], [1:160:2], [0:640:2]} | slice | bytes 3276800 | tf_op jit(solution)/shard_map/slice | solution.py:78
  112.7 56.6 %slice.30 = f32[16,80,320]{2,1,0:T(8,128)} slice(f32[16,160,640]{2,1,0:T(8,128)} %param.11), slice={[0:16:1], [0:160:2], [1:640:2]} | slice | bytes 3276800 | tf_op jit(solution)/shard_map/slice | solution.py:79
  169.2 56.7 %slice.31 = f32[16,80,320]{2,1,0:T(8,128)} slice(f32[16,160,640]{2,1,0:T(8,128)} %param.11), slice={[0:16:1], [1:160:2], [1:640:2]} | slice | bytes 3276800 | tf_op jit(solution)/shard_map/slice | solution.py:79
  227.4 11.2 sort.17
  246.9 94.0 %scatter_custom_fusion = s32[25600]{0:T(1024)S(1)} fusion(s32[25600]{0:T(1024)S(1)} %compare_select_fusion.1, s32[25600]{0:T(1024)S(1)} %iota.51, s32[]{:T(128)} %constant.129.clone.1), kind=kCustom, calls=%fused_computation.66 | custom fusion | bytes 102404 | tf_op jit(solution)/shard_map/scatter | solution.py:34
  341.5 70.3 %scatter_custom_fusion.1 = bf16[16,40960]{0,1:T(8,128)(2,1)} fusion(s32[25600]{0:T(1024)S(1)} %get-tuple-element.188, bf16[25600,16]{1,0:T(8,128)(2,1)} %bitcast.129, bf16[]{:T(256)} %constant.136.clone.1), kind=kCustom, calls=%fused_computation.41 | custom fusion | bytes 1311232 | tf_op jit(solution)/shard_map/scatter | solution.py:90
  427.8 23.1 %exponential_bitcast_fusion = f32[16,16,40960]{2,1,0:T(8,128)} fusion(bf16[1,16,16,40960]{3,2,1,0:T(8,128)(2,1)} %param.13), kind=kLoop, calls=%fused_computation.20 | loop fusion | flops 20971520 | bytes 62914560 | tf_op jit(solution)/shard_map/exp | solution.py:48
  458.9 14.0 broadcast_multiply_fusion
  476.5 13.7 broadcast.222.clone
  490.1 96.8 %while.29 = (s32[]{:T(128)}, f32[16,40960]{1,0:T(8,128)S(1)}, f32[16,16,40960]{2,1,0:T(8,128)}, f32[16,16,40960]{2,1,0:T(8,128)}, f32[16,16,40960]{2,1,0:T(8,128)}, /*index=5*/s32[]{:T(128)}, s32[]{:T(128)}) while((s32[]{:T(128)}, f32[16,40960]{1,0:T(8,128)S(1)}, f32[16,16,40960]{2,1,0:T(8,128)}, f32[16,16,40960]{2,1,0:T(8,128)}, ...), condition=%wide.region_9.10_spmd, body=%wide.region_8.9_spmd.sunk | while | flops 2621443 | bytes 13107293 | solution.py:52
  586.9 26.8 %slice.34 = f32[15,16,40960]{2,1,0:T(8,128)} slice(f32[16,16,40960]{2,1,0:T(8,128)} %get-tuple-element.138), slice={[1:16], [0:16], [0:40960]} | slice | bytes 78643200 | tf_op jit(solution)/shard_map/slice | solution.py:53
  613.8 13.9 broadcast.222.clone.1
  627.7 93.9 %while.30 = (s32[]{:T(128)}, f32[16,40960]{1,0:T(8,128)S(1)}, f32[16,16,40960]{2,1,0:T(8,128)}, f32[16,16,40960]{2,1,0:T(8,128)}, f32[16,16,40960]{2,1,0:T(8,128)}, /*index=5*/s32[]{:T(128)}, s32[]{:T(128)}) while((s32[]{:T(128)}, f32[16,40960]{1,0:T(8,128)S(1)}, f32[16,16,40960]{2,1,0:T(8,128)}, f32[16,16,40960]{2,1,0:T(8,128)}, ...), condition=%wide.region_7.8_spmd.clone, body=%wide.region_6.7_spmd.clone.sunk | while | flops 3276803 | bytes 13107799 | solution.py:50
  721.6 27.2 %slice.32 = f32[15,16,40960]{2,1,0:T(8,128)} slice(f32[16,16,40960]{2,1,0:T(8,128)} %get-tuple-element.137), slice={[0:15], [0:16], [0:40960]} | slice | bytes 78643200 | tf_op jit(solution)/shard_map/slice | solution.py:51
  748.8 50.9 %fusion.7 = bf16[16,40960]{1,0:T(8,128)(2,1)S(1)} fusion(f32[16,16,40960]{2,1,0:T(8,128)} %get-tuple-element.138, f32[1,16,40960]{2,1,0:T(8,128)S(1)} %copy-done.1, f32[15,16,40960]{2,1,0:T(8,128)} %slice.34, f32[16,16,40960]{2,1,0:T(8,128)} %get-tuple-element.137, f32[15,16,40960]{2,1,0:T(8,128)} %slice.32), kind=kLoop, calls=%fused_computation.19 | loop fusion | flops 51773440 | bytes 166461440 | tf_op jit(solution)/shard_map/reduce_sum | solution.py:54
  799.8 36.5 %all_to_all.53 = bf16[16,32,1280]{2,0,1:T(8,128)(2,1)S(1)} all-to-all(bf16[16,32,1280]{2,0,1:T(8,128)(2,1)S(1)} %bitcast.131), channel_id=1, replica_groups=mesh['lat'=8,'lon'=4] {'lat','lon'}, dimensions={1} | all-to-all | bytes 2621440 | tf_op jit(solution)/shard_map/all_to_all | solution.py:102
  842.8 91.6 %gather_fusion = bf16[25600,16]{1,0:T(8,128)(2,1)} fusion(bf16[16,40960]{0,1:T(8,128)(2,1)} %bitcast.121, s32[25600]{0:T(1024)S(1)} %copy-done.4), kind=kCustom, calls=%fused_computation | custom fusion | bytes 1740800 | tf_op jit(solution)/shard_map/gather | solution.py:109
  966.9 10.9 copy.96
  992.5 71.4 %all-to-all-done.2 = bf16[16,160,640]{2,1,0:T(8,128)(2,1)S(1)} async-done(((bf16[16,160,640]{2,1,0:T(8,128)(2,1)}), bf16[16,160,640]{2,1,0:T(8,128)(2,1)S(1)}, u32[]{:S(2)}, u32[]{:S(2)}) %all-to-all-start.2) | async-done | bytes 3276832 | tf_op jit(solution)/shard_map/all_to_all | solution.py:118
  1064.9 116.1 %select_convert_fusion = bf16[4,160,2560]{2,1,0:T(8,128)(2,1)S(1)} fusion(bf16[4,160,2560]{2,1,0:T(8,128)(2,1)S(1)} %bitcast.132, s32[2560]{0:T(1024)S(1)} %get-tuple-element.186, pred[2560]{0:T(1024)(128)(4,1)S(1)} %fusion.46, pred[160,2560]{1,0:T(8,128)(4,1)S(1)} %copy-done.3), kind=kOutput, calls=%fused_computation.39 | convolution fusion | flops 8470528000 | bytes 6976000 | tf_op jit(solution)/shard_map/dot_general | solution.py:121
  1199.3 114.2 %all-to-all-done.3 = bf16[32,4,160,80]{3,2,1,0:T(8,128)(2,1)} async-done(((bf16[32,4,160,80]{3,2,1,0:T(8,128)(2,1)}), bf16[32,4,160,80]{3,2,1,0:T(8,128)(2,1)}, u32[]{:S(2)}, u32[]{:S(2)}) %all-to-all-start.3) | async-done | bytes 3276832 | tf_op jit(solution)/shard_map/all_to_all | solution.py:129
  1313.5 10.4 copy.99
  1331.9 30.5 %fusion.26 = f32[1344,20,2,16,2]{0,3,4,2,1:T(8,128)} fusion(bf16[16,1280,20,2,2]{1,0,4,3,2:T(8,128)(2,1)S(1)} %reshape.269, bf16[20,1280,1344]{1,2,0:T(8,128)(2,1)} %param.16), kind=kOutput, calls=%fused_computation.43 | convolution fusion | flops 4404019200 | bytes 78970880 | tf_op jit(solution)/shard_map/syc,lyswp->cswlp/dot_general | solution.py:135
  1366.8 23.5 %fusion.39 = bf16[16,1280,20,2,2]{1,0,4,3,2:T(8,128)(2,1)S(1)} fusion(bf16[20,1280,1344]{1,2,0:T(8,128)(2,1)} %param.16, bf16[1344,20,1,16,2]{0,3,4,2,1:T(8,128)(2,1)S(1)} %broadcast_select_fusion, bf16[1344,20,1,16,2]{0,3,4,2,1:T(8,128)(2,1)S(1)} %get-tuple-element.181), kind=kOutput, calls=%fused_computation.51 | convolution fusion | flops 4407377920 | bytes 75530240 | tf_op jit(solution)/shard_map/syc,cswlp->lyswp/dot_general | solution.py:155
  1398.0 9.4 copy.100
  1407.4 121.4 %all_to_all.54 = bf16[32,4,160,80]{3,2,1,0:T(8,128)(2,1)S(1)} all-to-all(bf16[32,4,160,80]{3,2,1,0:T(8,128)(2,1)} %bitcast.124), channel_id=1, replica_groups=mesh['lat'=8,'lon'=4] {'lat','lon'}, dimensions={0} | all-to-all | bytes 6553600 | tf_op jit(solution)/shard_map/all_to_all | solution.py:162
  1534.5 9.6 dot_general.20
  1544.1 111.9 %fusion.14 = f32[4,160,2560]{2,1,0:T(8,128)} fusion(bf16[4,160,2560]{2,1,0:T(8,128)(2,1)S(1)} %dot_general.20, s32[2560]{0:T(1024)S(1)} %get-tuple-element.186, pred[2560]{0:T(1024)(128)(4,1)S(1)} %fusion.46), kind=kOutput, calls=%fused_computation.31 | convolution fusion | flops 8467251200 | bytes 9843200 | tf_op jit(solution)/shard_map/dot_general | solution.py:172
  1656.0 10.5 copy.102
  1666.5 237.3 %all_to_all.55 = f32[4,160,2560]{1,0,2:T(4,128)} all-to-all(f32[4,160,2560]{1,0,2:T(4,128)} %copy.102), channel_id=1, replica_groups=mesh['lat'=8,'lon'=4] {'lon'}, dimensions={2} | all-to-all | bytes 13107200 | tf_op jit(solution)/shard_map/all_to_all | solution.py:176
  1903.9 11.0 copy.103
  (98 shorter events, 327.2 us)
Async XLA Ops:
  56.1 169.8 %copy-start.2 = (s32[1,25600,1]{1,2,0:T(1,128)S(1)}, s32[1,25600,1]{1,2,0:T(1,128)}, u32[]{:S(2)}) copy-start(s32[1,25600,1]{1,2,0:T(1,128)} %param.12) | copy-start | bytes 307204
  420.4 38.0 %all-to-all-start = ((bf16[16,32,1280]{2,0,1:T(8,128)(2,1)}), bf16[16,32,1280]{2,0,1:T(8,128)(2,1)S(1)}, u32[]{:S(2)}, u32[]{:S(2)}) async-start(bf16[16,32,1280]{2,0,1:T(8,128)(2,1)} %copy.90), calls=%async_computation | async-start | bytes 2621440 | tf_op jit(solution)/shard_map/all_to_all | solution.py:92
  613.8 13.9 copy-start
  721.6 27.2 %copy-start.1 = (f32[1,16,40960]{2,1,0:T(8,128)S(1)}, f32[1,16,40960]{2,1,0:T(8,128)}, u32[]{:S(2)}) copy-start(f32[1,16,40960]{2,1,0:T(8,128)} %get-tuple-element.189) | copy-start | bytes 7864324
  836.3 6.5 copy-start.4
  985.1 4.0 copy-start.5
  985.1 6.1 copy-start.7
  985.1 6.4 copy-start.6
  985.1 78.8 %all-to-all-start.2 = ((bf16[16,160,640]{2,1,0:T(8,128)(2,1)}), bf16[16,160,640]{2,1,0:T(8,128)(2,1)S(1)}, u32[]{:S(2)}, u32[]{:S(2)}) async-start(bf16[16,160,640]{2,1,0:T(8,128)(2,1)} %add_convert_fusion), calls=%async_computation.2 | async-start | bytes 6553600 | tf_op jit(solution)/shard_map/all_to_all | solution.py:118
  1063.9 1.0 copy-start.3
  1195.4 118.1 %all-to-all-start.3 = ((bf16[32,4,160,80]{3,2,1,0:T(8,128)(2,1)}), bf16[32,4,160,80]{3,2,1,0:T(8,128)(2,1)}, u32[]{:S(2)}, u32[]{:S(2)}) async-start(bf16[32,4,160,80]{3,2,1,0:T(8,128)(2,1)} %bitcast.122), calls=%async_computation.3 | async-start | bytes 10485760 | tf_op jit(solution)/shard_map/all_to_all | solution.py:129
where the time goes:
time: 1930 us; the launch traced here: 1920 us
  local copies, waits for them, and re-layouts  713 us (37%)
  blocking collectives  395 us (20%)
  other arithmetic  317 us (16%)
  matrix products  282 us (15%)
  waiting for transfers between devices  193 us (10%)
    all_to_all x1, blocking collectives, per_device(): lax.all_to_all(lat_grid, 'lon', split_axis=2, concat_axis=0, tiled=True)  237 us
    dynamic_update_slice x32, other arithmetic, radiate(): _, below = lax.scan(flux_step, jnp.zeros_like(planck[0]), (passing, planck))  191 us
    all_to_all x1, blocking collectives, per_device(): lax.all_to_all(back_rows.reshape(devices_all, level_group, parallel_circl...  121 us
    dot_general x1, matrix products, per_device(): jnp.dot(piece.reshape(-1, nlon), full_table, preferred_element_type=jnp.f...  116 us
    all_to_all x1, waiting for transfers between devices, per_device(): lax.all_to_all(flat_send, ('lat', 'lon'), split_axis=0, concat_axis=0, ti...  114 us
    dot_general x1, matrix products, per_device(): lax.dot_general(row_synth, full_table, (((1,), (1,)), ((), ())), preferre...  112 us
    scatter x1, local copies, waits for them, and re-layouts, owner_ranks(): jnp.zeros_like(owner).at[order]  94 us
    gather x1, local copies, waits for them, and re-layouts, per_device(): returned.reshape(vertical_layer_pile, devices_all * capacity)[:, slots]  91.6 us
  transfers between devices with their start and end apart: 3, of which 3 were waited for; matrix products, arithmetic and copies ran while one was open for 1% of the time, Pallas kernels for 0%

commit v1 on v0

v1 whole, which is shorter than its diff:
```python
import math

import jax
import jax.numpy as jnp
from jax import lax
from jax.experimental import pallas as pl
from jax.experimental.pallas import tpu as pltpu
from jax.sharding import PartitionSpec as P

DIFFUSION = 4.0


def wave_numbers(pairs, nwave):
    repeated = jnp.repeat(pairs, 4)
    which = jnp.tile(jnp.array([0, 0, 1, 1], dtype=jnp.int32), pairs.shape[0])
    return jnp.where(which == 0, repeated, nwave - 1 - repeated)


def turn_angles(places, waves, nlon):
    phase = places[:, None] * waves[None, :] % nlon
    return phase.astype(jnp.float32) * (2.0 * math.pi / nlon)


def dft_table(waves, nlon):
    fine = 32
    while nlon % fine:
        fine //= 2
    high = turn_angles(jnp.arange(nlon // fine, dtype=jnp.int32) * fine, waves, nlon)
    low = turn_angles(jnp.arange(fine, dtype=jnp.int32), waves, nlon)
    even = (jnp.arange(waves.shape[0], dtype=jnp.int32) % 2 == 0)[None, :]
    scale = 1.0 / math.sqrt(nlon)
    cos_high, sin_high = jnp.cos(high) * scale, jnp.sin(high) * scale
    with_cos = jnp.where(even, cos_high, sin_high)
    with_sin = jnp.where(even, -sin_high, cos_high)
    with_cos, with_sin, cos_low, sin_low = lax.optimization_barrier(
        (with_cos, with_sin, jnp.cos(low), jnp.sin(low))
    )
    table = with_cos[:, None] * cos_low[None] + with_sin[:, None] * sin_low[None]
    table = table.astype(jnp.bfloat16).reshape(nlon, waves.shape[0])
    return lax.optimization_barrier(table)


def owner_ranks(owner, devices_all):
    matches = (owner[:, None] == jnp.arange(devices_all, dtype=jnp.int32)[None, :]).astype(
        jnp.int32
    )
    counts = jnp.sum(matches, axis=0)
    starts = jnp.cumsum(counts) - counts
    start_each = jnp.sum(matches * starts[None, :], axis=1)
    position = jnp.argsort(jnp.argsort(owner, stable=True))
    return position.astype(jnp.int32) - start_each


def radiate_kernel(temp_ref, depth_ref, out_ref, source_ref, heat_ref):
    layers, bands, width = depth_ref.shape
    chunk = 256 if width % 256 == 0 else 128
    source_ref[...] = jnp.exp(0.5 * temp_ref[...].astype(jnp.float32))

    def columns(i, carry):
        part = pl.ds(pl.multiple_of(i * chunk, chunk), chunk)
        band = lax.broadcasted_iota(jnp.int32, (bands, chunk), 0).astype(jnp.float32)
        weights = (band + 1.0) * (2.0 / (bands * (bands + 1)))
        taken = [
            1.0 - jnp.exp(-depth_ref[l, :, part].astype(jnp.float32)) for l in range(layers)
        ]
        planck = lambda l: weights * source_ref[l : l + 1, part]
        flux = jnp.zeros((bands, chunk), jnp.float32)
        sums = []
        for l in range(layers):
            change = taken[l] * (flux - planck(l))
            flux = flux - change
            sums.append(change)
        flux = planck(layers - 1)
        for l in reversed(range(layers)):
            change = taken[l] * (flux - planck(l))
            flux = flux - change
            heat_ref[l : l + 1, part] = jnp.sum(sums[l] + change, axis=0, keepdims=True)
        return carry

    lax.fori_loop(0, width // chunk, columns, 0)
    out_ref[...] = heat_ref[...].astype(jnp.bfloat16)


def radiate(column_temp, depth):
    layers, bands, total = depth.shape
    width = 2048
    while total % width:
        width //= 2
    return pl.pallas_call(
        radiate_kernel,
        grid=(total // width,),
        out_shape=jax.ShapeDtypeStruct((layers, total), jnp.bfloat16),
        in_specs=[
            pl.BlockSpec((layers, width), lambda i: (0, i)),
            pl.BlockSpec((layers, bands, width), lambda i: (0, 0, i)),
        ],
        out_specs=pl.BlockSpec((layers, width), lambda i: (0, i)),
        scratch_shapes=[pltpu.VMEM((layers, width), jnp.float32)] * 2,
        compiler_params=pltpu.CompilerParams(vmem_limit_bytes=24 << 20),
        cost_estimate=pl.CostEstimate(
            flops=12 * layers * bands * total,
            bytes_accessed=2 * layers * bands * total,
            transcendentals=layers * bands * total,
        ),
    )(column_temp, depth)


def pool_kernel(grid_ref, rows_ref, cols_ref, out_ref):
    high = lax.Precision.HIGHEST
    kept = jnp.float32
    lines = jnp.dot(rows_ref[...], grid_ref[0], precision=high, preferred_element_type=kept)
    tiles = jnp.dot(lines, cols_ref[...], precision=high, preferred_element_type=kept)
    out_ref[0] = (tiles * 0.25).astype(jnp.bfloat16)


def halves(coarse, dtype):
    fine = jnp.arange(2 * coarse, dtype=jnp.int32) // 2
    return (jnp.arange(coarse, dtype=jnp.int32)[:, None] == fine[None, :]).astype(dtype)


def pool(grid):
    layers, lines, places = grid.shape
    rows, cols = lines // 2, places // 2
    return pl.pallas_call(
        pool_kernel,
        grid=(layers,),
        out_shape=jax.ShapeDtypeStruct((layers, rows, cols), jnp.bfloat16),
        in_specs=[
            pl.BlockSpec((1, lines, places), lambda l: (l, 0, 0)),
            pl.BlockSpec((rows, lines), lambda l: (0, 0)),
            pl.BlockSpec((places, cols), lambda l: (0, 0)),
        ],
        out_specs=pl.BlockSpec((1, rows, cols), lambda l: (l, 0, 0)),
        compiler_params=pltpu.CompilerParams(vmem_limit_bytes=24 << 20),
    )(grid, halves(rows, jnp.float32), halves(cols, jnp.float32).T)


def force_kernel(grid_ref, heat_ref, rows_ref, cols_ref, out_ref):
    wide = jnp.dot(heat_ref[0], cols_ref[...], preferred_element_type=jnp.float32)
    full = jnp.dot(
        rows_ref[...], wide.astype(jnp.bfloat16), preferred_element_type=jnp.float32
    )
    out_ref[0] = (grid_ref[0] + full).astype(jnp.bfloat16)


def force(grid, heat):
    layers, lines, places = grid.shape
    rows, cols = lines // 2, places // 2
    return pl.pallas_call(
        force_kernel,
        grid=(layers,),
        out_shape=jax.ShapeDtypeStruct((layers, lines, places), jnp.bfloat16),
        in_specs=[
            pl.BlockSpec((1, lines, places), lambda l: (l, 0, 0)),
            pl.BlockSpec((1, rows, cols), lambda l: (l, 0, 0)),
            pl.BlockSpec((lines, rows), lambda l: (0, 0)),
            pl.BlockSpec((cols, places), lambda l: (0, 0)),
        ],
        out_specs=pl.BlockSpec((1, lines, places), lambda l: (l, 0, 0)),
        compiler_params=pltpu.CompilerParams(vmem_limit_bytes=24 << 20),
    )(grid, heat, halves(rows, jnp.bfloat16).T, halves(cols, jnp.bfloat16))


def per_device(
    gaussian_thermal_state,
    radiation_holder_device,
    layer_opacity_depths,
    wavenumber_duos_placed,
    reduced_grid_sites,
    weighted_polynomial_basis,
):
    vertical_layer_pile, parallel_circle_lines, meridian_entries = gaussian_thermal_state.shape
    group = weighted_polynomial_basis.shape[0]
    nlat_all = weighted_polynomial_basis.shape[1]
    ndeg = weighted_polynomial_basis.shape[2]
    nwave = wavenumber_duos_placed.shape[0] * 2
    nlon = nwave * 2
    lat_size = lax.axis_size("lat")
    lon_size = lax.axis_size("lon")
    devices_all = lat_size * lon_size
    capacity = layer_opacity_depths.shape[3] // devices_all
    level_group = vertical_layer_pile // lon_size
    coarse_rows, coarse_cols = parallel_circle_lines // 2, meridian_entries // 2
    column_temp = pool(gaussian_thermal_state).reshape(
        vertical_layer_pile, coarse_rows * coarse_cols
    )
    owner = radiation_holder_device[0, :, 0]
    slots = owner * capacity + owner_ranks(owner, devices_all)
    outgoing = (
        jnp.zeros((vertical_layer_pile, devices_all * capacity), jnp.bfloat16)
        .at[:, slots]
        .set(column_temp)
    )
    arrived = lax.all_to_all(
        outgoing.reshape(vertical_layer_pile, devices_all, capacity),
        ("lat", "lon"),
        split_axis=1,
        concat_axis=1,
        tiled=True,
    )
    heating = radiate(
        arrived.reshape(vertical_layer_pile, devices_all * capacity), layer_opacity_depths[0]
    )
    returned = lax.all_to_all(
        heating.reshape(vertical_layer_pile, devices_all, capacity),
        ("lat", "lon"),
        split_axis=1,
        concat_axis=1,
        tiled=True,
    )
    column_heat = returned.reshape(vertical_layer_pile, devices_all * capacity)[:, slots].reshape(
        vertical_layer_pile, coarse_rows, coarse_cols
    )
    radiatively_driven_thermal = force(gaussian_thermal_state, column_heat)
    all_waves = wave_numbers(wavenumber_duos_placed, nwave)
    full_table = dft_table(all_waves, nlon)
    piece = lax.all_to_all(
        radiatively_driven_thermal, "lon", split_axis=0, concat_axis=2, tiled=True
    )
    points = level_group * parallel_circle_lines
    product = lax.dot_general(
        full_table,
        piece.reshape(points, nlon),
        (((0,), (1,)), ((), ())),
        preferred_element_type=jnp.float32,
    )
    keep_all = 2 * all_waves[:, None] < jnp.tile(reduced_grid_sites, level_group)[None, :]
    row_fourier = jnp.where(keep_all, product, 0.0).astype(jnp.bfloat16)
    gathered = lax.all_to_all(
        row_fourier.reshape(devices_all, 4 * group, points),
        ("lat", "lon"),
        split_axis=0,
        concat_axis=0,
        tiled=True,
    ).reshape(lat_size, lon_size, group, 4, level_group, parallel_circle_lines)
    fourier = gathered.transpose(2, 3, 1, 4, 0, 5).reshape(
        group, 4 * vertical_layer_pile, nlat_all
    )
    device_index = lax.axis_index("lat") * lon_size + lax.axis_index("lon")
    my_pairs = lax.dynamic_slice_in_dim(wavenumber_duos_placed, device_index * group, group)
    full = lax.dot_general(
        fourier,
        weighted_polynomial_basis,
        (((2,), (1,)), ((0,), (0,))),
        preferred_element_type=jnp.float32,
    )
    coeff = jnp.arange(ndeg, dtype=jnp.int32)[None, :]
    first = coeff < (nwave - my_pairs)[:, None]
    degree = jnp.where(first, my_pairs[:, None] + coeff, coeff - 1).astype(jnp.float32)
    factor = jnp.where(
        coeff <= nwave,
        1.0 / (1.0 + DIFFUSION * degree * (degree + 1.0) / (nwave * nwave)),
        0.0,
    )
    side = jnp.arange(4 * vertical_layer_pile, dtype=jnp.int32) < 2 * vertical_layer_pile
    chosen = first[:, None, :] == side[None, :, None]
    split = jnp.where(chosen, full * factor[:, None, :], 0.0).astype(jnp.bfloat16)
    synth = lax.dot_general(
        split,
        weighted_polynomial_basis,
        (((2,), (2,)), ((0,), (0,))),
        preferred_element_type=jnp.float32,
    ).astype(jnp.bfloat16)
    back = synth.reshape(
        group, 4, lon_size, level_group, lat_size, parallel_circle_lines
    ).transpose(4, 2, 0, 1, 3, 5)
    row_synth = lax.all_to_all(
        back.reshape(devices_all, 4 * group, points),
        ("lat", "lon"),
        split_axis=0,
        concat_axis=0,
        tiled=True,
    ).reshape(devices_all * 4 * group, points)
    lat_grid = lax.dot_general(
        row_synth, full_table, (((0,), (1,)), ((), ())), preferred_element_type=jnp.float32
    ).astype(jnp.bfloat16)
    lat_grid = lat_grid.reshape(level_group, parallel_circle_lines, nlon)
    tile = lax.all_to_all(lat_grid, "lon", split_axis=2, concat_axis=0, tiled=True)
    return tile.astype(jnp.float32)


def solution(mesh):
    in_specs = (
        P(None, "lat", "lon"),
        P(("lat", "lon"), None, None),
        P(("lat", "lon"), None, None, None),
        P(),
        P("lat"),
        P(("lat", "lon"), None, None),
    )
    out_specs = P(None, "lat", "lon")
    return jax.shard_map(
        per_device, mesh=mesh, in_specs=in_specs, out_specs=out_specs, check_vma=False
    )
```

time: 1930 us -> 877 us (0.45)
  local copies, waits for them, and re-layouts: 713 us -> 271 us
  other arithmetic: 317 us -> 47 us
  matrix products: 282 us -> 77.8 us
  blocking collectives: 395 us -> 241 us
  Pallas kernels: 0 us -> 54.6 us
  waiting for transfers between devices: 193 us -> 163 us
    slice x7 -> x0, local copies, waits for them, and re-layouts: 283 us -> none  [the longest x1 56.7 us: per_device(): gaussian_thermal_state[:, 1::2, 1::2]]
    dot_general x4, matrix products: 282 us -> 77.8 us  [the longest x1 28.3 us: per_device(): lax.dot_general(fourier, weighted_polynomial_basis, (((2,), (1,)), ((0,),...]
    dynamic_update_slice x32 -> x0, other arithmetic: 191 us -> none  [radiate(): _, below = lax.scan(flux_step, jnp.zeros_like(planck[0]), (passing, planck))]
    all_to_all x1, blocking collectives: 237 us -> 123 us  [per_device(): lax.all_to_all(lat_grid, 'lon', split_axis=2, concat_axis=0, tiled=True)]
    scatter x1 -> x0, local copies, waits for them, and re-layouts: 94 us -> none  [owner_ranks(): jnp.zeros_like(owner).at[order]]
    pallas_call x0 -> x3, Pallas kernels: none -> 54.6 us  [the longest x1 30.7 us: radiate(): pl.pallas_call(radiate_kernel, grid=(total // width,), out_shape=jax.Shap...]
    reduce_sum x1 -> x0, other arithmetic: 50.9 us -> none  [radiate(): return jnp.sum(above - below + under - upper, axis=1)]
    all_to_all x2, blocking collectives: 158 us -> 119 us  [the longest x1 79.8 us: per_device(): lax.all_to_all(back.reshape(devices_all, 4 * group, points), ('lat', 'lon...]
  transfers between devices with their start and end apart: 3 -> 3, of which waited for: 3 -> 3; matrix products, arithmetic and copies ran while one was open for 1% -> 2% of each run, Pallas kernels for 0% -> 0%
where the time goes in v1:
time: 877 us; the launch traced here: 866 us
  local copies, waits for them, and re-layouts  271 us (31%)
  blocking collectives  241 us (27%)
  waiting for transfers between devices  163 us (19%)
  matrix products  77.8 us (9%)
  Pallas kernels  54.6 us (6%)
  other arithmetic  47 us (5%)
  starting transfers between devices  11.3 us (1%)
    all_to_all x1, blocking collectives, per_device(): lax.all_to_all(lat_grid, 'lon', split_axis=2, concat_axis=0, tiled=True)  123 us
    gather x1, local copies, waits for them, and re-layouts, per_device(): returned.reshape(vertical_layer_pile, devices_all * capacity)[:, slots]  91.6 us
    all_to_all x1, blocking collectives, per_device(): lax.all_to_all(back.reshape(devices_all, 4 * group, points), ('lat', 'lon...  79.8 us
    all_to_all x1, waiting for transfers between devices, per_device(): lax.all_to_all(row_fourier.reshape(devices_all, 4 * group, points), ('lat...  72.6 us
    scatter x1, local copies, waits for them, and re-layouts, per_device(): outgoing = jnp.zeros((vertical_layer_pile, devices_all * capacity), jnp.b...  70.7 us
    all_to_all x1, waiting for transfers between devices, per_device(): lax.all_to_all(radiatively_driven_thermal, 'lon', split_axis=0, concat_ax...  60.1 us
    all_to_all x1, blocking collectives, per_device(): lax.all_to_all(outgoing.reshape(vertical_layer_pile, devices_all, capacit...  39.1 us
    pallas_call x1, Pallas kernels, radiate(): pl.pallas_call(radiate_kernel, grid=(total // width,), out_shape=jax.Shap...  30.7 us
  transfers between devices with their start and end apart: 3, of which 3 were waited for; matrix products, arithmetic and copies ran while one was open for 2% of the time, Pallas kernels for 0%

profile of v1, /device:TPU:0, one launch (start us, length us, event | category | flops | bytes accessed | tf_op | source)
XLA Modules:
  0.0 866.3 jit_solution(16052325331316528499)
XLA Ops:
  3.3 12.0 %sort.34 = (s32[25600]{0:T(1024)}, s32[25600]{0:T(1024)S(1)}) sort(s32[25600]{0:T(1024)} %bitcast.74, s32[25600]{0:T(1024)S(1)} %iota.85), dimensions={0}, to_apply=%region_0.1 | sort | flops 384000 | bytes 409600 | tf_op jit(solution)/shard_map/jit(argsort)/sort | solution.py:50
  18.3 15.2 %shard_map.73 = bf16[16,80,320]{2,1,0:T(8,128)(2,1)S(1)} custom-call(f32[16,160,640]{2,1,0:T(8,128)S(1)} %copy-done, f32[80,160]{1,0:T(8,128)S(1)} %fusion.17.rows_ref, f32[640,320]{1,0:T(8,128)S(1)} %fusion.2.cols_ref), custom_call_target="tpu_custom_call" | custom-call | tf_op jit(solution)/shard_map/pallas_call | solution.py:124
  33.5 4.8 copy.55
  38.3 11.3 %sort.35 = (s32[25600]{0:T(1024)}, s32[25600]{0:T(1024)S(1)}) sort(s32[25600]{0:T(1024)S(1)} %get-tuple-element.15, s32[25600]{0:T(1024)S(1)} %iota.86), dimensions={0}, to_apply=%region_1.2 | sort | flops 384000 | bytes 409600 | tf_op jit(solution)/shard_map/jit(argsort)/sort | solution.py:50
  49.6 70.7 %scatter_custom_fusion = bf16[16,40960]{0,1:T(8,128)(2,1)} fusion(s32[25600]{0:T(1024)S(1)} %get-tuple-element.22, bf16[25600,16]{1,0:T(8,128)(2,1)} %bitcast.66, bf16[]{:T(256)} %constant.108.clone.1), kind=kCustom, calls=%fused_computation.7 | custom fusion | bytes 1311232 | tf_op jit(solution)/shard_map/scatter | solution.py:192
  120.3 7.5 copy.45
  127.7 39.1 %all_to_all.44 = bf16[16,32,1280]{2,0,1:T(8,128)(2,1)S(1)} all-to-all(bf16[16,32,1280]{2,0,1:T(8,128)(2,1)S(1)} %copy.45), channel_id=1, replica_groups=mesh['lat'=8,'lon'=4] {'lat','lon'}, dimensions={1} | all-to-all | bytes 2621440 | tf_op jit(solution)/shard_map/all_to_all | solution.py:194
  166.9 7.0 copy-done.2
  173.9 30.7 %shard_map.74 = bf16[16,40960]{1,0:T(8,128)(2,1)S(1)} custom-call(bf16[16,40960]{1,0:T(8,128)(2,1)S(1)} %bitcast.54, bf16[16,16,40960]{2,1,0:T(8,128)(2,1)S(1)} %bitcast.53), custom_call_target="tpu_custom_call" | custom-call | flops 125829120 | bytes 20971520 | tf_op jit(solution)/shard_map/pallas_call | solution.py:89
  209.3 30.3 %all-to-all-done.1 = bf16[16,32,1280]{2,0,1:T(8,128)(2,1)S(1)} async-done(((bf16[16,32,1280]{2,0,1:T(8,128)(2,1)}), bf16[16,32,1280]{2,0,1:T(8,128)(2,1)S(1)}, u32[]{:S(2)}, u32[]{:S(2)}) %all-to-all-start.1) | async-done | bytes 1310752 | tf_op jit(solution)/shard_map/all_to_all | solution.py:204
  239.7 6.5 copy.48
  246.2 91.6 %gather_fusion = bf16[25600,16]{1,0:T(8,128)(2,1)} fusion(bf16[16,40960]{0,1:T(8,128)(2,1)} %bitcast.57, s32[25600]{0:T(1024)S(1)} %get-tuple-element.21), kind=kCustom, calls=%fused_computation | custom fusion | bytes 1740800 | tf_op jit(solution)/shard_map/gather | solution.py:211
  337.8 5.5 copy.56.heat_ref
  346.2 8.7 %shard_map.75 = bf16[16,160,640]{2,1,0:T(8,128)(2,1)} custom-call(f32[16,160,640]{2,1,0:T(8,128)S(1)} %copy-done.1, bf16[16,80,320]{2,1,0:T(8,128)(2,1)S(1)} %copy.56.heat_ref, bf16[160,80]{1,0:T(8,128)(2,1)S(1)} %fusion.18.rows_ref, bf16[320,640]{1,0:T(8,128)(2,1)S(1)} %fusion.8.cols_ref), custom_call_target="tpu_custom_call" | custom-call | tf_op jit(solution)/shard_map/pallas_call | solution.py:149
  366.9 7.3 add_convert_fusion
  374.2 60.1 %all-to-all-done.2 = bf16[16,160,640]{2,1,0:T(8,128)(2,1)S(1)} async-done(((bf16[16,160,640]{2,1,0:T(8,128)(2,1)}), bf16[16,160,640]{2,1,0:T(8,128)(2,1)S(1)}, u32[]{:S(2)}, u32[]{:S(2)}) %all-to-all-start.2) | async-done | bytes 3276832 | tf_op jit(solution)/shard_map/all_to_all | solution.py:217
  439.1 12.7 %select_convert_fusion.1 = bf16[2560,640]{1,0:T(8,128)(2,1)} fusion(bf16[2560,2560]{1,0:T(8,128)(2,1)S(1)} %bitcast.64, bf16[640,2560]{1,0:T(8,128)(2,1)S(1)} %bitcast.69, s32[640]{0:T(1024)S(1)} %lt.81, s32[2560]{0:T(1024)S(1)} %get-tuple-element.19), kind=kOutput, calls=%fused_computation.5 | convolution fusion | flops 8393523200 | bytes 19673600 | tf_op jit(solution)/shard_map/dot_general | solution.py:221
  455.4 72.6 %all-to-all-done.3 = bf16[32,80,640]{2,1,0:T(8,128)(2,1)S(1)} async-done(((bf16[32,80,640]{2,1,0:T(8,128)(2,1)}), bf16[32,80,640]{2,1,0:T(8,128)(2,1)S(1)}, u32[]{:S(2)}, u32[]{:S(2)}) %all-to-all-start.3) | async-done | bytes 3276832 | tf_op jit(solution)/shard_map/all_to_all | solution.py:229
  528.0 5.5 reshape.271
  533.5 10.4 %copy.51 = bf16[20,4,4,4,8,160]{5,4,3,2,1,0:T(8,128)(2,1)} copy(bf16[20,4,4,4,8,160]{5,3,1,0,2,4:T(4,128)(2,1)} %bitcast.58) | data formatting | bytes 6553600 | tf_op jit(solution)/shard_map/transpose | solution.py:236
  543.9 8.0 reshape.272
  551.9 28.3 %select_convert_fusion.clone.4 = bf16[20,64,1344]{2,1,0:T(8,128)(2,1)} fusion(bf16[20,64,1280]{2,1,0:T(8,128)(2,1)S(1)} %reshape.272, bf16[20,1280,1344]{1,2,0:T(8,128)(2,1)} %param.12, f32[20,1344]{1,0:T(8,128)S(1)} %divide_select_fusion, pred[20,1344]{1,0:T(8,128)(4,1)S(1)} %iota_compare_fusion.3, pred[64]{0:T(512)(128)(4,1)S(1)} %iota_compare_fusion.7), kind=kOutput, calls=%fused_computation.4.clone.clone.clone.1 | convolution fusion | flops 4410900480 | bytes 75664704 | tf_op jit(solution)/shard_map/dot_general | solution.py:241
  580.2 24.9 %convolution_convert_fusion.1 = bf16[20,64,1280]{2,1,0:T(8,128)(2,1)S(1)} fusion(bf16[20,1280,1344]{1,2,0:T(8,128)(2,1)} %param.12, bf16[20,64,1344]{2,1,0:T(8,128)(2,1)} %select_convert_fusion.clone.4), kind=kOutput, calls=%fused_computation.10 | convolution fusion | flops 4405657600 | bytes 75530240 | tf_op jit(solution)/shard_map/dot_general | solution.py:258
  605.2 7.9 reshape.273
  613.1 7.5 copy.62
  620.6 6.8 reshape.274
  627.4 79.8 %all_to_all.45 = bf16[32,80,640]{2,1,0:T(8,128)(2,1)S(1)} all-to-all(bf16[32,80,640]{2,1,0:T(8,128)(2,1)S(1)} %reshape.274), channel_id=1, replica_groups=mesh['lat'=8,'lon'=4] {'lat','lon'}, dimensions={0} | all-to-all | bytes 6553600 | tf_op jit(solution)/shard_map/all_to_all | solution.py:267
  707.3 11.8 %convolution_convert_fusion = bf16[640,2560]{1,0:T(8,128)(2,1)S(1)} fusion(bf16[2560,640]{1,0:T(8,128)(2,1)S(1)} %bitcast.70, bf16[2560,2560]{1,0:T(8,128)(2,1)} %bitcast.63), kind=kOutput, calls=%fused_computation.9 | convolution fusion | flops 8390246400 | bytes 19660800 | tf_op jit(solution)/shard_map/dot_general | solution.py:274
  719.0 5.7 copy.53
  724.7 122.5 %all_to_all.46 = bf16[4,160,2560]{1,0,2:T(4,128)(2,1)} all-to-all(bf16[4,160,2560]{1,0,2:T(4,128)(2,1)} %copy.53), channel_id=1, replica_groups=mesh['lat'=8,'lon'=4] {'lon'}, dimensions={2} | all-to-all | bytes 6553600 | tf_op jit(solution)/shard_map/all_to_all | solution.py:278
  847.2 7.8 convert_bitcast_fusion
  855.1 11.0 %copy.54 = f32[4,4,160,640]{3,2,1,0:T(8,128)} copy(f32[4,4,160,640]{2,1,3,0:T(4,128)} %convert_bitcast_fusion) | data formatting | bytes 13107200 | tf_op jit(solution)/shard_map/convert_element_type | solution.py:279
  (54 shorter events, 34.1 us)
Async XLA Ops:
  15.4 2.9 copy-start
  18.3 31.3 %copy-start.4 = (s32[1,25600,1]{1,2,0:T(1,128)S(1)}, s32[1,25600,1]{1,2,0:T(1,128)}, u32[]{:S(2)}) copy-start(s32[1,25600,1]{1,2,0:T(1,128)} %param.8) | copy-start | bytes 307204
  166.9 7.0 copy-start.2
  205.7 33.9 %all-to-all-start.1 = ((bf16[16,32,1280]{2,0,1:T(8,128)(2,1)}), bf16[16,32,1280]{2,0,1:T(8,128)(2,1)S(1)}, u32[]{:S(2)}, u32[]{:S(2)}) async-start(bf16[16,32,1280]{2,0,1:T(8,128)(2,1)} %bitcast.51), calls=%async_computation.1 | async-start | bytes 2621440 | tf_op jit(solution)/shard_map/all_to_all | solution.py:204
  343.3 2.9 copy-start.1
  346.2 13.5 %copy-start.6 = (s32[160]{0:T(256)S(1)}, s32[160]{0:T(256)}, u32[]{:S(2)}) copy-start(s32[160]{0:T(256)} %param.11) | copy-start | bytes 1924
  346.2 13.6 %copy-start.7 = (pred[4]{0:T(512)(128)(4,1)S(1)}, pred[4]{0:T(512)(128)(4,1)}, u32[]{:S(2)}) copy-start(pred[4]{0:T(512)(128)(4,1)} %constant.119) | copy-start | bytes 16
  346.2 13.8 %copy-start.5 = (s32[640]{0:T(1024)S(1)}, s32[640]{0:T(1024)}, u32[]{:S(2)}) copy-start(s32[640]{0:T(1024)} %param.10) | copy-start | bytes 7684
  354.9 79.4 %all-to-all-start.2 = ((bf16[16,160,640]{2,1,0:T(8,128)(2,1)}), bf16[16,160,640]{2,1,0:T(8,128)(2,1)S(1)}, u32[]{:S(2)}, u32[]{:S(2)}) async-start(bf16[16,160,640]{2,1,0:T(8,128)(2,1)} %shard_map.75), calls=%async_computation.2 | async-start | bytes 6553600 | tf_op jit(solution)/shard_map/all_to_all | solution.py:217
  434.4 4.7 copy-start.3
  451.8 76.1 %all-to-all-start.3 = ((bf16[32,80,640]{2,1,0:T(8,128)(2,1)}), bf16[32,80,640]{2,1,0:T(8,128)(2,1)S(1)}, u32[]{:S(2)}, u32[]{:S(2)}) async-start(bf16[32,80,640]{2,1,0:T(8,128)(2,1)} %bitcast.68), calls=%async_computation.3 | async-start | bytes 6553600 | tf_op jit(solution)/shard_map/all_to_all | solution.py:229
